TPU v7x, 32 devices: a whole 2x2x4 slice. The times are simulated.
32 devices in a mesh: fsdp: 8 (over z, x), sp: 4 (over y, core).
Axes of the slice: x: 2, y: 2, z: 4, core: 2. Of those that a mesh axis runs over, the one named last changes fastest.
Arguments:
- tokens: bfloat16 [8, 512, 5120], P('fsdp', 'sp'), may hold values from -32 to 32
- w_query: bfloat16 [5120, 2560], P('fsdp', 'sp'), may hold values from -1 to 1
- w_key: bfloat16 [5120, 2560], P('fsdp', 'sp'), may hold values from -1 to 1
- values: bfloat16 [8, 512, 2560], P('fsdp', 'sp'), may hold values from -6 to 6
- grad_out: bfloat16 [8, 512, 2560], P('fsdp', 'sp'), may hold values from -6 to 6
- kv_index: int32 [8, 20, 4, 4], P('fsdp', 'sp'), may hold values from 0 to 3, as said below
- kv_count: int32 [8, 20, 4], P('fsdp', 'sp'), may hold values from 1 to 4, as said below
Outputs:
- grad_tokens: bfloat16 [8, 512, 5120], P('fsdp', 'sp')
- grad_values: bfloat16 [8, 512, 2560], P('fsdp', 'sp')
- grad_wq: float32 [5120, 2560], P('fsdp', 'sp')
- grad_wk: float32 [5120, 2560], P('fsdp', 'sp')
Inputs may be any that keep to these rules, and one draw needn't show every extreme that they name: Each row kv_index[b, h, i, :] is a permutation of 0 to 3 whose first entry is i. Only the first kv_count[b, h, i] entries of row kv_index[b, h, i, :] are live; the rest are ignored.
All inputs are finite; a program needn't handle non-finite values.
Results may differ from a plain program's by a relative error of at most 0.015.
The roundings to bfloat16 on the way count: a program that leaves them out, or rounds other values in their place, can miss the bound.
Values may be sent and summed in bfloat16 or wider, within the bound.
A program may use at most 128 MiB of HBM per device.

v0:
```python
import math

import jax
import jax.numpy as jnp
from jax import lax
from jax.sharding import PartitionSpec as P

HEAD_DIM = 128
BLOCK = 128


def live_blocks(kv_index, kv_count):
    nblocks = kv_index.shape[-1]
    slot_ids = jnp.arange(nblocks, dtype=jnp.int32)
    in_use = slot_ids[None, None, :] < kv_count[:, :, None]
    matches = (kv_index[:, :, :, None] == slot_ids[None, None, None, :]) & in_use[:, :, :, None]
    return jnp.any(matches, axis=2)


def attend_back(query, keys, values, upstream, live):
    length = query.shape[0]
    count_heads = live.shape[0]
    scale = 1.0 / math.sqrt(HEAD_DIM)
    query_h = query.reshape(length, count_heads, HEAD_DIM)
    keys_h = keys.reshape(length, count_heads, HEAD_DIM)
    values_h = values.reshape(length, count_heads, HEAD_DIM)
    upstream_h = upstream.reshape(length, count_heads, HEAD_DIM)
    scores = jnp.einsum("qhd,khd->hqk", query_h, keys_h, preferred_element_type=jnp.float32) * scale
    token_live = jnp.repeat(jnp.repeat(live, BLOCK, axis=1), BLOCK, axis=2)
    scores = jnp.where(token_live, scores, -jnp.inf)
    row_max = jnp.max(scores, axis=2, keepdims=True)
    expon = jnp.exp(scores - row_max)
    probs = expon / jnp.sum(expon, axis=2, keepdims=True)
    probs_low = probs.astype(jnp.bfloat16)
    dprob = jnp.einsum("qhd,khd->hqk", upstream_h, values_h, preferred_element_type=jnp.float32)
    delta = jnp.sum(probs * dprob, axis=2, keepdims=True)
    dscore = (probs * (dprob - delta) * scale).astype(jnp.bfloat16)
    grad_q = jnp.einsum("hqk,khd->qhd", dscore, keys_h, preferred_element_type=jnp.float32).astype(
        jnp.bfloat16
    )
    grad_k = jnp.einsum("hqk,qhd->khd", dscore, query_h, preferred_element_type=jnp.float32).astype(
        jnp.bfloat16
    )
    grad_v = jnp.einsum(
        "hqk,qhd->khd", probs_low, upstream_h, preferred_element_type=jnp.float32
    ).astype(jnp.bfloat16)
    return (grad_q.reshape(length, -1), grad_k.reshape(length, -1), grad_v.reshape(length, -1))


def contract_rows(left, right):
    return lax.dot_general(
        left, right, (((1,), (1,)), ((), ())), preferred_element_type=jnp.float32
    )


def weight_term(whole_x, grads):
    return lax.dot_general(
        whole_x, grads, (((0,), (0,)), ((), ())), preferred_element_type=jnp.float32
    )


def local(tokens, w_query, w_key, values, grad_out, kv_index, kv_count):
    local_x = tokens[0]
    whole_x = lax.all_gather(local_x, "sp", axis=0, tiled=True)
    full_query, full_key = (
        lax.all_gather(w_query, "fsdp", axis=0, tiled=True),
        lax.all_gather(w_key, "fsdp", axis=0, tiled=True),
    )
    head_values, head_upstream = (
        lax.all_to_all(values[0], "sp", split_axis=1, concat_axis=0, tiled=True),
        lax.all_to_all(grad_out[0], "sp", split_axis=1, concat_axis=0, tiled=True),
    )
    query = jnp.dot(whole_x, full_query, preferred_element_type=jnp.float32).astype(jnp.bfloat16)
    keys = jnp.dot(whole_x, full_key, preferred_element_type=jnp.float32).astype(jnp.bfloat16)
    live = live_blocks(kv_index[0], kv_count[0])
    grad_q, grad_k, grad_v = attend_back(query, keys, head_values, head_upstream, live)
    token_values = lax.all_to_all(grad_v, "sp", split_axis=0, concat_axis=1, tiled=True)
    partial_x = contract_rows(grad_q, full_query) + contract_rows(grad_k, full_key)
    grad_x = lax.psum_scatter(partial_x.astype(jnp.bfloat16), "sp", scatter_dimension=0, tiled=True)
    grad_wq = lax.psum_scatter(
        weight_term(whole_x, grad_q).astype(jnp.bfloat16), "fsdp", scatter_dimension=0, tiled=True
    ).astype(jnp.float32)
    grad_wk = lax.psum_scatter(
        weight_term(whole_x, grad_k).astype(jnp.bfloat16), "fsdp", scatter_dimension=0, tiled=True
    ).astype(jnp.float32)
    return (grad_x[None], token_values[None], grad_wq, grad_wk)


def solution(mesh):
    in_specs = (
        P("fsdp", "sp", None),
        P("fsdp", "sp"),
        P("fsdp", "sp"),
        P("fsdp", "sp", None),
        P("fsdp", "sp", None),
        P("fsdp", "sp", None, None),
        P("fsdp", "sp", None),
    )
    out_specs = (P("fsdp", "sp", None), P("fsdp", "sp", None), P("fsdp", "sp"), P("fsdp", "sp"))
    return jax.shard_map(local, mesh=mesh, in_specs=in_specs, out_specs=out_specs, check_vma=False)
```

profile of v0, /device:TPU:8, one launch (start us, length us, event | category | flops | bytes accessed | tf_op | source)
XLA Modules:
  0.0 615.3 jit_solution(17751584307204388556)
XLA Ops:
  7.2 0.0 copy-start.1
  7.2 0.0 copy-start.3
  7.2 0.0 copy-start.2
  7.2 0.0 all-gather.9.cloned.1.call-start
  7.2 0.7 all-gather.9.cloned.1.call-update
  7.9 0.0 all-gather.5.cloned.1.call-start
  8.0 0.7 all-gather.5.cloned.1.call-update
  8.7 0.0 all-gather.7.cloned.1.call-start
  8.7 0.7 all-gather.7.cloned.1.call-update
  9.4 2.2 copy.82
  11.6 3.5 all-to-all-start.1
  15.1 0.0 copy-done.1
  15.1 1.1 copy.80
  16.2 13.3 %all-to-all-done.1 = bf16[128,4,640]{0,2,1:T(8,128)(2,1)S(1)} async-done(((bf16[128,4,640]{0,2,1:T(8,128)(2,1)}), bf16[128,4,640]{0,2,1:T(8,128)(2,1)S(1)}, u32[]{:S(2)}, u32[]{:S(2)}) %all-to-all-start.1) | async-done | bytes 655392 | tf_op jit(solution)/shard_map/all_to_all | solution.py:70
  29.4 3.5 all-to-all-start
  32.9 0.0 reduce-scatter.10.cloned.1.call-start
  33.0 0.0 copy-done.3
  33.0 0.0 copy-done.2
  33.0 0.1 copy.76
  33.2 0.1 broadcast_in_dim.22
  33.3 0.5 copy.83
  33.8 0.2 reshape.61
  34.1 16.4 %all-to-all-done = bf16[128,4,640]{0,2,1:T(8,128)(2,1)S(1)} async-done(((bf16[128,4,640]{0,2,1:T(8,128)(2,1)}), bf16[128,4,640]{0,2,1:T(8,128)(2,1)S(1)}, u32[]{:S(2)}, u32[]{:S(2)}) %all-to-all-start) | async-done | bytes 655392 | tf_op jit(solution)/shard_map/all_to_all | solution.py:71
  50.5 0.5 copy.81
  51.0 0.2 reshape.60
  51.2 3.1 fusion.48
  54.4 7.7 %all-gather.9.cloned.1.call-done = bf16[1,512,5120]{2,1,0:T(8,128)(2,1)} async-done(((bf16[1,128,5120]{2,1,0:T(8,128)(2,1)}), bf16[1,512,5120]{2,1,0:T(8,128)(2,1)}) %all-gather.9.cloned.1.call-update) | async-done | bytes 5242896 | tf_op jit(solution)/shard_map/all_gather | solution.py:64
  62.0 103.1 %all-gather.5.cloned.1.call-done = bf16[5120,640]{1,0:T(8,128)(2,1)} async-done(((bf16[640,640]{1,0:T(8,128)(2,1)}), bf16[5120,640]{1,0:T(8,128)(2,1)}) %all-gather.5.cloned.1.call-update) | async-done | bytes 6553616 | tf_op jit(solution)/shard_map/all_gather | solution.py:67
  165.2 8.6 %fusion.32 = bf16[512,640]{1,0:T(8,128)(2,1)S(1)} fusion(bf16[5120,640]{1,0:T(8,128)(2,1)} %all-gather.5.cloned.1.call-done, bf16[1,512,5120]{2,1,0:T(8,128)(2,1)} %all-gather.9.cloned.1.call-done), kind=kOutput, calls=%fused_computation.28 | convolution fusion | flops 3355770880 | bytes 12451840 | tf_op jit(solution)/shard_map/dot_general | solution.py:74
  173.8 0.3 copy.75
  174.1 93.7 %all-gather.7.cloned.1.call-done = bf16[5120,640]{1,0:T(8,128)(2,1)} async-done(((bf16[640,640]{1,0:T(8,128)(2,1)}), bf16[5120,640]{1,0:T(8,128)(2,1)}) %all-gather.7.cloned.1.call-update) | async-done | bytes 6553616 | tf_op jit(solution)/shard_map/all_gather | solution.py:66
  267.8 8.6 %fusion.35 = bf16[512,640]{1,0:T(8,128)(2,1)S(1)} fusion(bf16[5120,640]{1,0:T(8,128)(2,1)} %all-gather.7.cloned.1.call-done, bf16[1,512,5120]{2,1,0:T(8,128)(2,1)} %all-gather.9.cloned.1.call-done), kind=kOutput, calls=%fused_computation.29 | convolution fusion | flops 3355770880 | bytes 12451840 | tf_op jit(solution)/shard_map/dot_general | solution.py:73
  276.4 0.3 copy.77
  276.7 0.9 multiply_select_fusion
  277.6 0.0 copy-start
  277.6 3.9 fusion.47
  281.5 0.1 copy-done
  281.6 9.5 %fusion.26 = bf16[5,128,512]{2,1,0:T(8,128)(2,1)S(1)} fusion(bf16[512,5,128]{0,2,1:T(8,128)(2,1)S(1)} %bitcast.69, f32[5,512,512]{1,2,0:T(8,128)} %fusion.48, f32[5,512,512]{1,2,0:T(8,128)} %get-tuple-element.25, f32[5,512]{1,0:T(8,128)S(1)} %get-tuple-element.24), kind=kOutput, calls=%fused_computation.26 | convolution fusion | flops 345050112 | bytes 11806720 | tf_op jit(solution)/shard_map/hqk,khd->qhd/dot_general | solution.py:38
  291.1 8.1 %fusion.2 = bf16[5120,640]{0,1:T(8,128)(2,1)} fusion(bf16[512,640]{0,1:T(8,128)(2,1)S(1)} %bitcast.76, bf16[1,512,5120]{2,1,0:T(8,128)(2,1)} %all-gather.9.cloned.1.call-done), kind=kOutput, calls=%fused_computation.5 | convolution fusion | flops 3358720000 | bytes 12451840 | tf_op jit(solution)/shard_map/dot_general | solution.py:57
  299.2 9.5 %copy.101 = bf16[5120,640]{1,0:T(8,128)(2,1)} copy(bf16[5120,640]{0,1:T(8,128)(2,1)} %fusion.2) | data formatting | bytes 13107200
  308.7 0.0 reduce-scatter.10.cloned.1.call-update
  308.7 0.0 reduce-scatter.12.cloned.1.call-start
  308.7 8.1 %fusion.29 = bf16[5,128,512]{2,1,0:T(8,128)(2,1)S(1)} fusion(bf16[512,5,128]{0,2,1:T(8,128)(2,1)S(1)} %bitcast.67, f32[5,512,512]{1,2,0:T(8,128)} %fusion.48, f32[5,512,512]{1,2,0:T(8,128)} %get-tuple-element.25, f32[5,512]{1,0:T(8,128)S(1)} %get-tuple-element.24), kind=kOutput, calls=%fused_computation.27 | convolution fusion | flops 345050112 | bytes 11806720 | tf_op jit(solution)/shard_map/hqk,qhd->khd/dot_general | solution.py:41
  316.9 8.0 %fusion.3 = bf16[5120,640]{0,1:T(8,128)(2,1)} fusion(bf16[512,640]{0,1:T(8,128)(2,1)S(1)} %bitcast.78, bf16[1,512,5120]{2,1,0:T(8,128)(2,1)} %all-gather.9.cloned.1.call-done), kind=kOutput, calls=%fused_computation.6 | convolution fusion | flops 3358720000 | bytes 12451840 | tf_op jit(solution)/shard_map/dot_general | solution.py:57
  324.9 9.5 %copy.103 = bf16[5120,640]{1,0:T(8,128)(2,1)} copy(bf16[5120,640]{0,1:T(8,128)(2,1)} %fusion.3) | data formatting | bytes 13107200
  334.4 0.0 reduce-scatter.12.cloned.1.call-update
  334.4 0.3 reduce-scatter.8.cloned.1.call-start
  334.7 9.8 %fusion.49 = f32[512,5120]{1,0:T(8,128)} fusion(bf16[512,640]{0,1:T(8,128)(2,1)S(1)} %bitcast.77, bf16[5120,640]{1,0:T(8,128)(2,1)} %all-gather.7.cloned.1.call-done), kind=kOutput, calls=%fused_computation.41 | convolution fusion | flops 3355443200 | bytes 17694720 | tf_op jit(solution)/shard_map/dot_general | solution.py:51
  344.5 10.8 %add_convert_fusion = bf16[512,5120]{1,0:T(8,128)(2,1)} fusion(f32[512,5120]{1,0:T(8,128)} %fusion.49, bf16[512,640]{0,1:T(8,128)(2,1)S(1)} %bitcast.79, bf16[5120,640]{1,0:T(8,128)(2,1)} %all-gather.5.cloned.1.call-done), kind=kOutput, calls=%fused_computation.2 | convolution fusion | flops 3360686080 | bytes 22937600 | tf_op jit(solution)/shard_map/dot_general | solution.py:51
  355.3 0.0 reduce-scatter.8.cloned.1.call-update
  355.3 5.6 fusion.38
  361.0 0.2 copy.89
  361.2 0.2 all_to_all.42
  361.4 0.1 copy.90
  361.5 12.8 %all_to_all.48 = bf16[4,128,640]{1,2,0:T(8,128)(2,1)S(1)} all-to-all(bf16[4,128,640]{1,2,0:T(8,128)(2,1)S(1)} %copy.90), channel_id=1, replica_groups=mesh['fsdp'=8,'sp'=4] {'sp'}, dimensions={0} | all-to-all | bytes 1310720 | tf_op jit(solution)/shard_map/all_to_all | solution.py:77
  374.3 1.1 copy.91
  375.4 54.1 %reduce-scatter.10.cloned.1.call-done = bf16[640,640]{1,0:T(8,128)(2,1)} async-done(((bf16[5120,640]{1,0:T(8,128)(2,1)}), bf16[640,640]{1,0:T(8,128)(2,1)}) %reduce-scatter.10.cloned.1.call-update) | async-done | bytes 819216
  429.5 1.8 copy.102
  431.3 1.5 copy.92
  432.8 121.4 %reduce-scatter.12.cloned.1.call-done = bf16[640,640]{1,0:T(8,128)(2,1)} async-done(((bf16[5120,640]{1,0:T(8,128)(2,1)}), bf16[640,640]{1,0:T(8,128)(2,1)}) %reduce-scatter.12.cloned.1.call-update) | async-done | bytes 819216
  554.2 1.8 copy.104
  556.0 1.5 copy.93
  557.5 50.9 %reduce-scatter.8.cloned.1.call-done = bf16[128,5120]{1,0:T(8,128)(2,1)} async-done(((bf16[512,5120]{1,0:T(8,128)(2,1)}), bf16[128,5120]{1,0:T(8,128)(2,1)}) %reduce-scatter.8.cloned.1.call-update) | async-done | bytes 1310736 | tf_op jit(solution)/shard_map/reduce_scatter | solution.py:79
  (3 shorter events, 0.1 us)
Async XLA Ops:
  7.2 7.9 %copy-start.1 = (bf16[1,128,2560]{2,1,0:T(8,128)(2,1)S(1)}, bf16[1,128,2560]{2,1,0:T(8,128)(2,1)}, u32[]{:S(2)}) copy-start(bf16[1,128,2560]{2,1,0:T(8,128)(2,1)} %param.11) | copy-start | bytes 1966084
  7.2 25.8 %copy-start.3 = (s32[1,5,4]{1,2,0:T(4,128)S(1)}, s32[1,5,4]{1,2,0:T(4,128)}, u32[]{:S(2)}) copy-start(s32[1,5,4]{1,2,0:T(4,128)} %param.13) | copy-start | bytes 244
  7.2 25.8 %copy-start.2 = (s32[1,5,4,4]{1,3,2,0:T(4,128)S(1)}, s32[1,5,4,4]{1,3,2,0:T(4,128)}, u32[]{:S(2)}) copy-start(s32[1,5,4,4]{1,3,2,0:T(4,128)} %param.12) | copy-start | bytes 964
  7.2 54.9 %all-gather.9.cloned.1.call-start = ((), (), s32[]{:S(2)}) async-start(), calls=%async_computation.9 | async-start | bytes 6553600 | tf_op jit(solution)/shard_map/all_gather | solution.py:64
  7.9 157.2 %all-gather.5.cloned.1.call-start = ((), (), s32[]{:S(2)}) async-start(), calls=%async_computation.6 | async-start | bytes 7372800 | tf_op jit(solution)/shard_map/all_gather | solution.py:67
  8.7 259.1 %all-gather.7.cloned.1.call-start = ((), (), s32[]{:S(2)}) async-start(), calls=%async_computation.7 | async-start | bytes 7372800 | tf_op jit(solution)/shard_map/all_gather | solution.py:66
  11.6 17.9 %all-to-all-start.1 = ((bf16[128,4,640]{0,2,1:T(8,128)(2,1)}), bf16[128,4,640]{0,2,1:T(8,128)(2,1)S(1)}, u32[]{:S(2)}, u32[]{:S(2)}) async-start(bf16[128,4,640]{0,2,1:T(8,128)(2,1)} %bitcast.8), calls=%async_computation.1 | async-start | bytes 1310720 | tf_op jit(solution)/shard_map/all_to_all | solution.py:70
  29.4 21.0 %all-to-all-start = ((bf16[128,4,640]{0,2,1:T(8,128)(2,1)}), bf16[128,4,640]{0,2,1:T(8,128)(2,1)S(1)}, u32[]{:S(2)}, u32[]{:S(2)}) async-start(bf16[128,4,640]{0,2,1:T(8,128)(2,1)} %bitcast.6), calls=%async_computation | async-start | bytes 1310720 | tf_op jit(solution)/shard_map/all_to_all | solution.py:71
  32.9 396.5 %reduce-scatter.10.cloned.1.call-start = ((), (), s32[]{:S(2)}) async-start(), calls=%async_computation.10 | async-start | bytes 7372800
  277.6 4.0 copy-start
  308.7 245.5 %reduce-scatter.12.cloned.1.call-start = ((), (), s32[]{:S(2)}) async-start(), calls=%async_computation.11 | async-start | bytes 7372800
  334.4 274.0 %reduce-scatter.8.cloned.1.call-start = ((), (), s32[]{:S(2)}) async-start(), calls=%async_computation.8 | async-start | bytes 6553600 | tf_op jit(solution)/shard_map/reduce_scatter | solution.py:79
Sparse Core Ops, SparseCore 0:
  9.6 52.4 all-gather.8
  64.2 100.8 all-gather.4
  167.4 100.3 all-gather.6
  308.8 120.6 reduce-scatter.9
  433.4 120.7 reduce-scatter.11
  557.1 51.2 reduce-scatter.7
where the time goes:
time: 618 us; the launch traced here: 615 us
  waiting for transfers between devices  463 us (75%)
  matrix products  81.3 us (13%)
  local copies, waits for them, and re-layouts  32.9 us (5%)
  between operations  14.3 us (2%)
  blocking collectives  12.8 us (2%)
  starting transfers between devices  7.43 us (1%)
    unnamed x8, waiting for transfers between devices  178 us
    all_gather x1, waiting for transfers between devices, local(): lax.all_gather(w_key, 'fsdp', axis=0, tiled=True)  103 us
    all_gather x1, waiting for transfers between devices, local(): lax.all_gather(w_query, 'fsdp', axis=0, tiled=True)  93.7 us
    reduce_scatter x1, waiting for transfers between devices, local(): lax.psum_scatter(partial_x.astype(jnp.bfloat16), 'sp', scatter_dimension=...  50.9 us
    unnamed x17, local copies, waits for them, and re-layouts  30.1 us
    dot_general x2, matrix products, contract_rows(): lax.dot_general(left, right, (((1,), (1,)), ((), ())), preferred_element_...  20.6 us
    all_to_all x1, waiting for transfers between devices, local(): lax.all_to_all(grad_out[0], 'sp', split_axis=1, concat_axis=0, tiled=True)  16.4 us
    dot_general x2, matrix products, weight_term(): lax.dot_general(whole_x, grads, (((0,), (0,)), ((), ())), preferred_eleme...  16.1 us
  transfers between devices with their start and end apart: 8, of which 8 were waited for; matrix products, arithmetic and copies ran while one was open for 13% of the time, Pallas kernels for 0%

commit v1 on v0

v1 whole, which is shorter than its diff:
```python
import functools
import math

import jax
import jax.numpy as jnp
from jax import lax
from jax.experimental import pallas as pl
from jax.experimental.pallas import tpu as pltpu
from jax.sharding import PartitionSpec as P

HEAD_DIM = 128
PARTS = 4
BF16 = jnp.bfloat16
F32 = jnp.float32


def remote(src, dst, send_sem, recv_sem, axis, target):
    return pltpu.make_async_remote_copy(
        src_ref=src,
        dst_ref=dst,
        send_sem=send_sem,
        recv_sem=recv_sem,
        device_id={axis: target},
        device_id_type=pl.DeviceIdType.MESH,
    )


def place(n_f):
    f = lax.axis_index("fsdp")
    s = lax.axis_index("sp")
    return n_f // 2, f // 2, f % 2, s


def greet(n_f, n_s):
    depth, z, x, s = place(n_f)
    barrier = pltpu.get_barrier_semaphore()

    def signal(axis, target):
        pl.semaphore_signal(
            barrier, inc=1, device_id={axis: target}, device_id_type=pl.DeviceIdType.MESH
        )

    for k in range(1, n_s):
        signal("sp", (s + k) % n_s)
    signal("fsdp", z * 2 + 1 - x)

    @pl.when(z > 0)
    def _():
        signal("fsdp", (z - 1) * 2 + x)

    @pl.when(z < depth - 1)
    def _():
        signal("fsdp", (z + 1) * 2 + x)

    inner = (z > 0).astype(jnp.int32) + (z < depth - 1).astype(jnp.int32)
    pl.semaphore_wait(barrier, n_s + inner)


def gather_kernel(
    n_f, n_s, tok, wq, wk, val, gout, full_x, full_q, full_k, full_v, full_g, xt_out,
    x_in, xt, up_s, dn_s, x_s, z_r, x_r, sp_s, sp_r, loc, work,
):
    depth, z, x, s = place(n_f)
    rows = wq.shape[0]
    half = rows // 2
    t = tok.shape[0]
    hc = full_v.shape[1]
    ins, outs = (wq, wk), (full_q, full_k)

    def piece(zz, xx, c):
        start = (zz * 2 + xx) * rows + (c % 2) * half
        return outs[c // 2].at[pl.ds(pl.multiple_of(start, 16), half)]

    def own(c):
        return ins[c // 2].at[pl.ds((c % 2) * half, half)]

    def to_x(src, zz, c):
        return remote(src, piece(zz, x, c), x_s.at[zz, c], x_r.at[zz, c], "fsdp", z * 2 + 1 - x)

    def to_up(src, zz, c):
        return remote(src, piece(zz, x, c), up_s.at[zz, c], z_r.at[zz, c], "fsdp", (z + 1) * 2 + x)

    def to_dn(src, zz, c):
        return remote(src, piece(zz, x, c), dn_s.at[zz, c], z_r.at[zz, c], "fsdp", (z - 1) * 2 + x)

    def sp_copies(k):
        j = (s + k) % n_s
        mine = pl.ds(pl.multiple_of(s * t, 16), t)
        cols = pl.ds(pl.multiple_of(j * hc, 128), hc)
        return [
            remote(src, dst, sp_s.at[i, k - 1], sp_r.at[i, k - 1], "sp", j)
            for i, (src, dst) in enumerate(
                (
                    (tok, full_x.at[mine]),
                    (val.at[:, cols], full_v.at[mine]),
                    (gout.at[:, cols], full_g.at[mine]),
                )
            )
        ]

    mine = pl.ds(pl.multiple_of(s * t, 16), t)
    my_cols = pl.ds(pl.multiple_of(s * hc, 128), hc)
    my_rows = pl.ds(pl.multiple_of((z * 2 + x) * rows, 16), rows)
    locals_ = [
        pltpu.make_async_copy(src, dst, loc.at[i])
        for i, (src, dst) in enumerate(
            (
                (tok, full_x.at[mine]),
                (val.at[:, my_cols], full_v.at[mine]),
                (gout.at[:, my_cols], full_g.at[mine]),
                (wq, full_q.at[my_rows]),
                (wk, full_k.at[my_rows]),
            )
        )
    ]
    greet(n_f, n_s)
    for c in range(PARTS):
        to_x(own(c), z, c).start()

        @pl.when(z < depth - 1)
        def _():
            to_up(own(c), z, c).start()

        @pl.when(z > 0)
        def _():
            to_dn(own(c), z, c).start()

    for k in range(1, n_s):
        for copy in sp_copies(k):
            copy.start()
    for copy in locals_:
        copy.start()

    def forward(d):
        for c in range(PARTS):

            @pl.when(z - d >= 0)
            def _():
                zz = z - d
                blk = piece(zz, x, c)
                to_up(blk, zz, c).wait_recv()

                @pl.when(z < depth - 1)
                def _():
                    to_up(blk, zz, c).start()

                to_x(blk, zz, c).start()

            @pl.when(z + d < depth)
            def _():
                zz = z + d
                blk = piece(zz, x, c)
                to_dn(blk, zz, c).wait_recv()

                @pl.when(z > 0)
                def _():
                    to_dn(blk, zz, c).start()

                to_x(blk, zz, c).start()

    @pl.loop(1, depth)
    def _(d):
        forward(d)

    for k in range(1, n_s):
        for copy in sp_copies(k):
            copy.wait()
    for copy in locals_:
        copy.wait()
    load = pltpu.make_async_copy(full_x, x_in, work.at[0])
    load.start()
    load.wait()

    @pl.loop(0, x_in.shape[1] // 128)
    def _(i):
        at = pl.ds(pl.multiple_of(i * 128, 128), 128)
        xt[at, :] = x_in[:, at].T

    store = pltpu.make_async_copy(xt, xt_out, work.at[1])
    store.start()

    @pl.loop(0, depth)
    def _(zz):
        for c in range(PARTS):
            other = piece(zz, 1 - x, c)
            remote(
                other, other, x_s.at[zz, c], x_r.at[zz, c], "fsdp", z * 2 + 1 - x
            ).wait_recv()
            to_x(own(c), zz, c).wait_send()

            @pl.when((zz <= z) & (z < depth - 1))
            def _():
                to_up(own(c), zz, c).wait_send()

            @pl.when((zz >= z) & (z > 0))
            def _():
                to_dn(own(c), zz, c).wait_send()

    store.wait()


def attend_kernel(idx, cnt, x, wq, wk, v, g, grad, grad_v, p_s, d_s):
    h = pl.program_id(0)
    nb = idx.shape[2]
    block = x.shape[0] // nb
    scale = 1.0 / math.sqrt(HEAD_DIM)
    both = jnp.dot(
        x[...], jnp.concatenate([wq[...], wk[...]], axis=1), preferred_element_type=F32
    ).astype(BF16)
    q, k = both[:, :HEAD_DIM], both[:, HEAD_DIM:]
    vv, gg = v[...], g[...]
    nt = (((1,), (1,)), ((), ()))
    tn = (((0,), (0,)), ((), ()))
    col = lax.broadcasted_iota(jnp.int32, (block, nb * block), 1) // block
    for i in range(nb):
        live = jnp.zeros(col.shape, jnp.bool_)
        for n in range(nb):
            j = jnp.where(n < cnt[h, i], idx[h, i, n], -1)
            live = live | (col == j)
        at = slice(i * block, (i + 1) * block)
        scores = lax.dot_general(q[at], k, nt, preferred_element_type=F32) * scale
        scores = jnp.where(live, scores, -jnp.inf)
        expon = jnp.exp(scores - jnp.max(scores, axis=1, keepdims=True))
        probs = expon / jnp.sum(expon, axis=1, keepdims=True)
        dprob = lax.dot_general(gg[at], vv, nt, preferred_element_type=F32)
        delta = jnp.sum(probs * dprob, axis=1, keepdims=True)
        p_s[at, :] = probs.astype(BF16)
        d_s[at, :] = (probs * (dprob - delta) * scale).astype(BF16)
    d = d_s[...]
    grad[0] = jnp.dot(d, k, preferred_element_type=F32).astype(BF16)
    grad[1] = lax.dot_general(d, q, tn, preferred_element_type=F32).astype(BF16)
    grad_v[...] = lax.dot_general(p_s[...], gg, tn, preferred_element_type=F32).astype(BF16)


def scatter_kernel(
    n_f, n_s, chunk, xt_h, full_q, full_k, grad, gv, gx_out, gv_out, gw_out,
    xt, wbuf, xsend, xrecv, own, zrecv, gx, gxr,
    x_s, x_r, z_s, z_r, sp_s, sp_r, work,
):
    depth, z, x, s = place(n_f)
    rows, cols = gw_out.shape[1], gw_out.shape[2]
    half = rows // 2
    t, width = gx_out.shape

    def w_copy(i, slot):
        at = pl.ds(pl.multiple_of(i * chunk, 128), chunk)
        return [
            pltpu.make_async_copy(src.at[at], wbuf.at[slot, w], work.at[1 + w, slot])
            for w, src in enumerate((full_q, full_k))
        ]

    load = pltpu.make_async_copy(xt_h, xt, work.at[0, 0])
    load.start()
    for copy in w_copy(0, 0):
        copy.start()

    def order(i):
        odd = i % 2
        return odd * (i // 2) + (1 - odd) * (depth - 1 - i // 2)

    def part(c):
        w = c // 2
        return w, pl.ds(pl.multiple_of((c % 2) * half, 16), half)

    def term(zz, xx, c):
        start = (zz * 2 + xx) * rows + (c % 2) * half
        at = pl.ds(pl.multiple_of(start, 16), half)
        return jnp.dot(xt[at, :], grad[c // 2], preferred_element_type=F32).astype(BF16)

    def to_x(zz, c):
        w, at = part(c)
        return remote(
            xsend.at[zz, w, at], xrecv.at[zz, w, at], x_s.at[zz, c], x_r.at[zz, c],
            "fsdp", z * 2 + 1 - x,
        )

    def to_z(zz, c, slot, target):
        w, at = part(c)
        return remote(
            own.at[zz, w, at], zrecv.at[slot, w, at], z_s.at[zz, c], z_r.at[slot, c],
            "fsdp", target * 2 + x,
        )

    def gv_copy(k):
        j = (s + k) % n_s
        return remote(
            gv.at[pl.ds(pl.multiple_of(j * t, 16), t)],
            gv_out.at[:, pl.ds(pl.multiple_of(s * cols, 128), cols)],
            sp_s.at[0, k - 1], sp_r.at[0, k - 1], "sp", j,
        )

    def gx_copy(k):
        j = (s + k) % n_s
        return remote(
            gx.at[pl.ds(pl.multiple_of(j * t, 16), t)], gxr.at[k - 1],
            sp_s.at[1, k - 1], sp_r.at[1, k - 1], "sp", j,
        )

    gv_own = pltpu.make_async_copy(
        gv.at[pl.ds(pl.multiple_of(s * t, 16), t)],
        gv_out.at[:, pl.ds(pl.multiple_of(s * cols, 128), cols)],
        work.at[0, 1],
    )
    gv_own.start()
    greet(n_f, n_s)
    for k in range(1, n_s):
        gv_copy(k).start()
    load.wait()

    @pl.loop(0, depth * PARTS)
    def _(i):
        zz, c = order(i // PARTS), i % PARTS
        w, at = part(c)
        xsend[zz, w, at, :] = term(zz, 1 - x, c)
        to_x(zz, c).start()

    @pl.loop(0, depth * PARTS)
    def _(i):
        zz, c = i // PARTS, i % PARTS
        w, at = part(c)
        own[zz, w, at, :] = term(zz, x, c)

    nt = (((1,), (1,)), ((), ()))
    chunks = width // chunk

    @pl.loop(0, chunks)
    def _(i):
        slot = i % 2
        for copy in w_copy(i, slot):
            copy.wait()

        @pl.when(i + 1 < chunks)
        def _():
            for copy in w_copy(i + 1, 1 - slot):
                copy.start()

        acc = lax.dot_general(grad[0], wbuf[slot, 0], nt, preferred_element_type=F32)
        acc += lax.dot_general(grad[1], wbuf[slot, 1], nt, preferred_element_type=F32)
        gx[:, pl.ds(pl.multiple_of(i * chunk, 128), chunk)] = acc.astype(BF16)

    for k in range(1, n_s):
        gx_copy(k).start()

    @pl.loop(0, depth * PARTS)
    def _(i):
        zz, c = order(i // PARTS), i % PARTS
        w, at = part(c)
        to_x(zz, c).wait_recv()
        more = ((zz > z) & (z > 0)) | ((zz < z) & (z < depth - 1))

        def paired():
            return own[zz, w, at, :].astype(F32) + xrecv[zz, w, at, :].astype(F32)

        @pl.when(more)
        def _():
            to_z(zz, c, zz, z).wait_recv()
            own[zz, w, at, :] = (paired() + zrecv[zz, w, at, :].astype(F32)).astype(BF16)

        @pl.when(jnp.logical_not(more) & (zz != z))
        def _():
            own[zz, w, at, :] = paired().astype(BF16)

        @pl.when(zz > z)
        def _():
            to_z(zz, c, zz, z + 1).start()

        @pl.when(zz < z)
        def _():
            last = jnp.where(zz == z - 1, depth, zz)
            to_z(zz, c, last, z - 1).start()

        @pl.when(zz == z)
        def _():
            gw_out[w, at, :] = paired()

    for k in range(1, n_s):
        gx_copy(k).wait_recv()

    @pl.loop(0, chunks)
    def _(i):
        at = pl.ds(pl.multiple_of(i * chunk, 128), chunk)
        acc = gx[pl.ds(pl.multiple_of(s * t, 16), t), at].astype(F32)
        for k in range(n_s - 1):
            acc += gxr[k, :, at].astype(F32)
        gx_out[:, at] = acc.astype(BF16)

    @pl.loop(0, PARTS)
    def _(c):
        w, at = part(c)

        @pl.when(z > 0)
        def _():
            to_z(z, c, z, z).wait_recv()
            gw_out[w, at, :] += zrecv[z, w, at, :].astype(F32)

        @pl.when(z < depth - 1)
        def _():
            to_z(z, c, depth, z).wait_recv()
            gw_out[w, at, :] += zrecv[depth, w, at, :].astype(F32)

    @pl.loop(0, depth * PARTS)
    def _(i):
        zz, c = i // PARTS, i % PARTS
        to_x(zz, c).wait_send()

        @pl.when(zz != z)
        def _():
            to_z(zz, c, zz, z).wait_send()

    for k in range(1, n_s):
        gx_copy(k).wait_send()
        gv_copy(k).wait()
    gv_own.wait()


def local(n_f, n_s, tokens, w_query, w_key, values, grad_out, kv_index, kv_count):
    t, width = tokens.shape[1:]
    rows, cols = w_query.shape
    length = t * n_s
    heads = cols // HEAD_DIM
    depth = n_f // 2
    hbm = pl.BlockSpec(memory_space=pl.ANY)
    vmem = pl.BlockSpec(memory_space=pltpu.VMEM)
    smem = pl.BlockSpec(memory_space=pltpu.SMEM)
    dma = pltpu.SemaphoreType.DMA
    shape = jax.ShapeDtypeStruct
    full_x, full_q, full_k, full_v, full_g, xt = pl.pallas_call(
        functools.partial(gather_kernel, n_f, n_s),
        out_shape=(
            shape((length, width), BF16),
            shape((width, cols), BF16),
            shape((width, cols), BF16),
            shape((length, cols), BF16),
            shape((length, cols), BF16),
            shape((width, length), BF16),
        ),
        in_specs=[hbm] * 5,
        out_specs=(hbm,) * 6,
        scratch_shapes=[
            pltpu.VMEM((length, width), BF16),
            pltpu.VMEM((width, length), BF16),
            dma((depth, PARTS)),
            dma((depth, PARTS)),
            dma((depth, PARTS)),
            dma((depth, PARTS)),
            dma((depth, PARTS)),
            dma((3, n_s - 1)),
            dma((3, n_s - 1)),
            dma((5,)),
            dma((2,)),
        ],
        compiler_params=pltpu.CompilerParams(
            collective_id=0, has_side_effects=True, vmem_limit_bytes=60 * 2**20
        ),
        name="gather",
    )(tokens[0], w_query, w_key, values[0], grad_out[0])

    grad, gv = pl.pallas_call(
        attend_kernel,
        grid=(heads,),
        out_shape=(shape((2, length, cols), BF16), shape((length, cols), BF16)),
        in_specs=[
            smem,
            smem,
            pl.BlockSpec((length, width), lambda h: (0, 0)),
            pl.BlockSpec((width, HEAD_DIM), lambda h: (0, h)),
            pl.BlockSpec((width, HEAD_DIM), lambda h: (0, h)),
            pl.BlockSpec((length, HEAD_DIM), lambda h: (0, h)),
            pl.BlockSpec((length, HEAD_DIM), lambda h: (0, h)),
        ],
        out_specs=(
            pl.BlockSpec((2, length, HEAD_DIM), lambda h: (0, 0, h)),
            pl.BlockSpec((length, HEAD_DIM), lambda h: (0, h)),
        ),
        scratch_shapes=[pltpu.VMEM((length, length), BF16), pltpu.VMEM((length, length), BF16)],
        compiler_params=pltpu.CompilerParams(vmem_limit_bytes=60 * 2**20),
        name="attend",
    )(kv_index[0], kv_count[0], full_x, full_q, full_k, full_v, full_g)

    chunk = 512 if width % 512 == 0 else 128
    gx, token_gv, gw = pl.pallas_call(
        functools.partial(scatter_kernel, n_f, n_s, chunk),
        out_shape=(
            shape((t, width), BF16),
            shape((t, cols * n_s), BF16),
            shape((2, rows, cols), F32),
        ),
        in_specs=[hbm, hbm, hbm, vmem, vmem],
        out_specs=(vmem, hbm, vmem),
        scratch_shapes=[
            pltpu.VMEM((width, length), BF16),
            pltpu.VMEM((2, 2, chunk, cols), BF16),
            pltpu.VMEM((depth, 2, rows, cols), BF16),
            pltpu.VMEM((depth, 2, rows, cols), BF16),
            pltpu.VMEM((depth, 2, rows, cols), BF16),
            pltpu.VMEM((depth + 1, 2, rows, cols), BF16),
            pltpu.VMEM((length, width), BF16),
            pltpu.VMEM((n_s - 1, t, width), BF16),
            dma((depth, PARTS)),
            dma((depth, PARTS)),
            dma((depth, PARTS)),
            dma((depth + 1, PARTS)),
            dma((2, n_s - 1)),
            dma((2, n_s - 1)),
            dma((3, 2)),
        ],
        compiler_params=pltpu.CompilerParams(
            collective_id=1, has_side_effects=True, vmem_limit_bytes=60 * 2**20
        ),
        name="scatter",
    )(xt, full_q, full_k, grad, gv)
    return (gx[None], token_gv[None], gw[0], gw[1])


def solution(mesh):
    in_specs = (
        P("fsdp", "sp", None),
        P("fsdp", "sp"),
        P("fsdp", "sp"),
        P("fsdp", "sp", None),
        P("fsdp", "sp", None),
        P("fsdp", "sp", None, None),
        P("fsdp", "sp", None),
    )
    out_specs = (P("fsdp", "sp", None), P("fsdp", "sp", None), P("fsdp", "sp"), P("fsdp", "sp"))
    return jax.shard_map(
        functools.partial(local, mesh.shape["fsdp"], mesh.shape["sp"]),
        mesh=mesh,
        in_specs=in_specs,
        out_specs=out_specs,
        check_vma=False,
    )
```

time: 618 us -> 349 us (0.56)
  waiting for transfers between devices: 463 us -> 0 us
  Pallas kernels: 0 us -> 339 us
  matrix products: 81.3 us -> 0 us
  local copies, waits for them, and re-layouts: 32.9 us -> 9.04 us
  between operations: 14.3 us -> 0.66 us
  blocking collectives: 12.8 us -> 0 us
  starting transfers between devices: 7.43 us -> 0 us
    pallas_call x0 -> x3, Pallas kernels: none -> 339 us  [the longest x1 169 us: local(): pl.pallas_call(functools.partial(scatter_kernel, n_f, n_s, chunk), out_sh...]
    all_gather x3 -> x0, waiting for transfers between devices: 205 us -> none  [the longest x1 103 us: local(): lax.all_gather(w_key, 'fsdp', axis=0, tiled=True)]
    unnamed x8 -> x0, waiting for transfers between devices: 178 us -> none
    dot_general x11 -> x0, matrix products: 81.3 us -> none  [the longest x2 20.6 us: contract_rows(): lax.dot_general(left, right, (((1,), (1,)), ((), ())), preferred_element_...]
    reduce_scatter x1 -> x0, waiting for transfers between devices: 50.9 us -> none  [local(): lax.psum_scatter(partial_x.astype(jnp.bfloat16), 'sp', scatter_dimension=...]
    all_to_all x2 -> x0, waiting for transfers between devices: 29.7 us -> none  [the longest x1 16.4 us: local(): lax.all_to_all(grad_out[0], 'sp', split_axis=1, concat_axis=0, tiled=True)]
    unnamed x17 -> x6, local copies, waits for them, and re-layouts: 30.1 us -> 2.35 us
    all_to_all x1 -> x0, blocking collectives: 12.8 us -> none  [local(): lax.all_to_all(grad_v, 'sp', split_axis=0, concat_axis=1, tiled=True)]
  transfers between devices with their start and end apart: 8 -> 0, of which waited for: 8 -> 0; matrix products, arithmetic and copies ran while one was open for 13% -> 0% of each run, Pallas kernels for 0% -> 0%
where the time goes in v1:
time: 349 us
  Pallas kernels  339 us (97%)
  local copies, waits for them, and re-layouts  9.04 us (3%)
    pallas_call x1, Pallas kernels, local(): pl.pallas_call(functools.partial(scatter_kernel, n_f, n_s, chunk), out_sh...  169 us
    pallas_call x1, Pallas kernels, local(): pl.pallas_call(functools.partial(gather_kernel, n_f, n_s), out_shape=(sha...  146 us
    pallas_call x1, Pallas kernels, local(): pl.pallas_call(attend_kernel, grid=(heads,), out_shape=(shape((2, length,...  23.9 us

profile of v1, /device:TPU:8, one launch (start us, length us, event | category | flops | bytes accessed | tf_op | source)
XLA Modules:
  0.0 348.6 jit_solution(4352745375240379255)
XLA Ops:
  0.6 1.4 copy.12.cnt
  2.0 1.4 copy.11.idx
  3.4 145.7 %gather.1 = (bf16[512,5120]{1,0:T(8,128)(2,1)}, bf16[5120,640]{1,0:T(8,128)(2,1)}, bf16[5120,640]{1,0:T(8,128)(2,1)}, bf16[512,640]{1,0:T(8,128)(2,1)}, bf16[512...) custom-call(bf16[128,5120]{1,0:T(8,128)(2,1)} %bitcast.11, bf16[640,640]{1,0:T(8,128)(2,1)} %wq.1, bf16[640,640]{1,0:T(8,128)(2,1)} %wk.1, ...), custom_call_target="tpu_custom_call" | custom-call | tf_op jit(solution)/shard_map/gather/pallas_call | solution.py:427
  149.1 23.9 %attend.1 = (bf16[2,512,640]{2,1,0:T(8,128)(2,1)}, bf16[512,640]{1,0:T(8,128)(2,1)}) custom-call(s32[5,4,4]{2,1,0:T(4,128)} %copy.11.idx, s32[5,4]{1,0:T(8,128)} %copy.12.cnt, bf16[512,5120]{1,0:T(8,128)(2,1)} %get-tuple-element.18.x, bf16[5120,640]{1,0:T(8,128)(2,1)} %get-tuple-element.16.wq.full_q, bf16[5120,640]{1,0:T(8,128)(2,1)} %get-tuple-element.17.wk.full_k, ...), custom_call_target="tpu_custom_call" | custom-call | tf_op jit(solution)/shard_map/attend/pallas_call | solution.py:458
  172.9 169.4 %scatter.1 = (bf16[128,5120]{1,0:T(8,128)(2,1)}, bf16[128,2560]{1,0:T(8,128)(2,1)}, f32[2,640,640]{2,1,0:T(8,128)}) custom-call(bf16[5120,512]{1,0:T(8,128)(2,1)} %get-tuple-element.15.xt_h, bf16[5120,640]{1,0:T(8,128)(2,1)} %get-tuple-element.16.wq.full_q, bf16[5120,640]{1,0:T(8,128)(2,1)} %get-tuple-element.17.wk.full_k, ...), custom_call_target="tpu_custom_call" | custom-call | tf_op jit(solution)/shard_map/scatter/pallas_call | solution.py:481
  342.3 0.0 copy-start
  342.3 3.9 %slice_bitcast_fusion = (f32[640,640]{1,0:T(8,128)}, f32[640,640]{1,0:T(8,128)}) fusion(f32[2,640,640]{2,1,0:T(8,128)} %get-tuple-element.25), kind=kLoop, calls=%fused_computation | loop fusion | bytes 6553600 | tf_op jit(solution)/shard_map/squeeze | solution.py:512
  346.3 0.0 copy-start.1
  346.3 0.0 copy-done
  346.3 1.1 copy.15
  347.3 0.5 copy-done.1
  347.8 0.8 copy.16
Async XLA Ops:
  342.3 4.0 %copy-start = (bf16[128,5120]{1,0:T(8,128)(2,1)S(1)}, bf16[128,5120]{1,0:T(8,128)(2,1)}, u32[]{:S(2)}) copy-start(bf16[128,5120]{1,0:T(8,128)(2,1)} %get-tuple-element.23) | copy-start | bytes 3932164
  346.3 1.5 copy-start.1

commit v2 on v1

--- a/solution.py
+++ b/solution.py
@@ -56,167 +56,236 @@
     pl.semaphore_wait(barrier, n_s + inner)
 
 
+def first_rows(rows):
+    return 32 * max(1, round(0.15 * rows / 32))
+
+
 def gather_kernel(
-    n_f, n_s, tok, wq, wk, val, gout, full_x, full_q, full_k, full_v, full_g, xt_out,
-    x_in, xt, up_s, dn_s, x_s, z_r, x_r, sp_s, sp_r, loc, work,
+    n_f, n_s, tok, wq, wk, val, gout, q_out, k_out, full_q, full_k, full_v, full_g, xt_out,
+    x_in, xt, land, acc, up_s, dn_s, z_r, x_s, x_r, xf_s, xf_r, sp_s, sp_r, loc, out_sem, work,
 ):
     depth, z, x, s = place(n_f)
     rows = wq.shape[0]
-    half = rows // 2
+    few = first_rows(rows)
+    half = (rows - few) // 2
     t = tok.shape[0]
     hc = full_v.shape[1]
-    ins, outs = (wq, wk), (full_q, full_k)
-
-    def piece(zz, xx, c):
-        start = (zz * 2 + xx) * rows + (c % 2) * half
-        return outs[c // 2].at[pl.ds(pl.multiple_of(start, 16), half)]
-
-    def own(c):
-        return ins[c // 2].at[pl.ds((c % 2) * half, half)]
-
-    def to_x(src, zz, c):
-        return remote(src, piece(zz, x, c), x_s.at[zz, c], x_r.at[zz, c], "fsdp", z * 2 + 1 - x)
-
-    def to_up(src, zz, c):
-        return remote(src, piece(zz, x, c), up_s.at[zz, c], z_r.at[zz, c], "fsdp", (z + 1) * 2 + x)
-
-    def to_dn(src, zz, c):
-        return remote(src, piece(zz, x, c), dn_s.at[zz, c], z_r.at[zz, c], "fsdp", (z - 1) * 2 + x)
+    ins = (wq, wk)
+    spans = [(c // 2, few + (c % 2) * half, half) for c in range(PARTS)]
+    early = [(w, 0, few) for w in range(2)]
+
+    def span(p):
+        return spans[p] if p < PARTS else early[(p - PARTS) % 2]
+
+    def side(p):
+        return 1 - x if p >= PARTS + 2 else x
+
+    def piece(zz, xx, p):
+        w, start, size = span(p)
+        at = (zz * 2 + xx) * rows + start
+        return land.at[w, pl.ds(pl.multiple_of(at, 16), size)]
+
+    def own(p):
+        w, start, size = span(p)
+        return ins[w].at[pl.ds(start, size)]
+
+    def to_x(src, zz, p):
+        return remote(src, piece(zz, x, p), x_s.at[zz, p], x_r.at[zz, p], "fsdp", z * 2 + 1 - x)
+
+    def early_x(w):
+        return remote(
+            own(PARTS + w), piece(z, x, PARTS + w), xf_s.at[w], xf_r.at[w], "fsdp", z * 2 + 1 - x
+        )
+
+    def to_z(src, zz, p, sems, step):
+        return remote(
+            src, piece(zz, side(p), p), sems.at[zz, p], z_r.at[zz, p], "fsdp", (z + step) * 2 + x
+        )
+
+    def send_z(src, zz, p, up, dn):
+        if up:
+
+            @pl.when(z < depth - 1)
+            def _():
+                to_z(src, zz, p, up_s, 1).start()
+
+        if dn:
+
+            @pl.when(z > 0)
+            def _():
+                to_z(src, zz, p, dn_s, -1).start()
+
+    mine = pl.ds(pl.multiple_of(s * t, 16), t)
+    my_cols = pl.ds(pl.multiple_of(s * hc, 128), hc)
+    my_rows = pl.ds(pl.multiple_of((z * 2 + x) * rows, 16), rows)
 
     def sp_copies(k):
         j = (s + k) % n_s
-        mine = pl.ds(pl.multiple_of(s * t, 16), t)
         cols = pl.ds(pl.multiple_of(j * hc, 128), hc)
         return [
             remote(src, dst, sp_s.at[i, k - 1], sp_r.at[i, k - 1], "sp", j)
             for i, (src, dst) in enumerate(
                 (
-                    (tok, full_x.at[mine]),
+                    (tok, x_in.at[mine]),
                     (val.at[:, cols], full_v.at[mine]),
                     (gout.at[:, cols], full_g.at[mine]),
                 )
             )
         ]
 
-    mine = pl.ds(pl.multiple_of(s * t, 16), t)
-    my_cols = pl.ds(pl.multiple_of(s * hc, 128), hc)
-    my_rows = pl.ds(pl.multiple_of((z * 2 + x) * rows, 16), rows)
     locals_ = [
         pltpu.make_async_copy(src, dst, loc.at[i])
         for i, (src, dst) in enumerate(
             (
-                (tok, full_x.at[mine]),
+                (tok, x_in.at[mine]),
                 (val.at[:, my_cols], full_v.at[mine]),
                 (gout.at[:, my_cols], full_g.at[mine]),
-                (wq, full_q.at[my_rows]),
-                (wk, full_k.at[my_rows]),
+                (wq, land.at[0, my_rows]),
+                (wk, land.at[1, my_rows]),
             )
         )
     ]
     greet(n_f, n_s)
-    for c in range(PARTS):
-        to_x(own(c), z, c).start()
-
-        @pl.when(z < depth - 1)
-        def _():
-            to_up(own(c), z, c).start()
-
-        @pl.when(z > 0)
-        def _():
-            to_dn(own(c), z, c).start()
-
+    for w in range(2):
+        early_x(w).start()
+    for p in range(PARTS):
+        to_x(own(p), z, p).start()
+        send_z(own(p), z, p, True, True)
+    for w in range(2):
+        send_z(own(PARTS + w), z, PARTS + w, True, True)
     for k in range(1, n_s):
         for copy in sp_copies(k):
             copy.start()
     for copy in locals_:
         copy.start()
+    for w in range(2):
+        other = piece(z, 1 - x, PARTS + 2 + w)
+        remote(other, other, xf_s.at[w], xf_r.at[w], "fsdp", z * 2 + 1 - x).wait_recv()
+        send_z(other, z, PARTS + 2 + w, True, True)
+    acc[...] = jnp.zeros_like(acc)
+
+    def both_ways(d, body):
+        @pl.when(z - d >= 0)
+        def _():
+            body(z - d, True)
+
+        @pl.when(z + d < depth)
+        def _():
+            body(z + d, False)
 
     def forward(d):
-        for c in range(PARTS):
-
-            @pl.when(z - d >= 0)
-            def _():
-                zz = z - d
-                blk = piece(zz, x, c)
-                to_up(blk, zz, c).wait_recv()
-
-                @pl.when(z < depth - 1)
-                def _():
-                    to_up(blk, zz, c).start()
-
-                to_x(blk, zz, c).start()
-
-            @pl.when(z + d < depth)
-            def _():
-                zz = z + d
-                blk = piece(zz, x, c)
-                to_dn(blk, zz, c).wait_recv()
-
-                @pl.when(z > 0)
-                def _():
-                    to_dn(blk, zz, c).start()
-
-                to_x(blk, zz, c).start()
-
-    @pl.loop(1, depth)
-    def _(d):
-        forward(d)
-
+        for p in range(PARTS + 4):
+
+            def body(zz, up):
+                blk = piece(zz, side(p), p)
+                to_z(blk, zz, p, up_s if up else dn_s, 0).wait_recv()
+                send_z(blk, zz, p, up, not up)
+                if p < PARTS:
+                    to_x(blk, zz, p).start()
+
+            both_ways(d, body)
+
+    def keep(zz, xx, w):
+        at = pl.ds(pl.multiple_of((zz * 2 + xx) * rows, 16), rows)
+        return pltpu.make_async_copy(
+            land.at[w, at], (full_q, full_k)[w].at[at], out_sem.at[zz * 2 + xx, w]
+        )
+
+    def project(zz, xx):
+        at = pl.ds(pl.multiple_of((zz * 2 + xx) * rows, 16), rows)
+        for w in range(2):
+            keep(zz, xx, w).start()
+            if rows % 128 == 0:
+                cols = pl.ds(pl.multiple_of((zz * 2 + xx) * rows, 128), rows)
+                acc[w] += jnp.dot(x_in[:, cols], land[w, at, :], preferred_element_type=F32)
+            else:
+                acc[w] += lax.dot_general(
+                    xt[at, :], land[w, at, :], (((0,), (0,)), ((), ())), preferred_element_type=F32
+                )
+
+    def take_x(zz):
+        for p in range(PARTS):
+            other = piece(zz, 1 - x, p)
+            remote(
+                other, other, x_s.at[zz, p], x_r.at[zz, p], "fsdp", z * 2 + 1 - x
+            ).wait_recv()
+        project(zz, 1 - x)
+
+    forward(1)
     for k in range(1, n_s):
         for copy in sp_copies(k):
             copy.wait()
     for copy in locals_:
         copy.wait()
-    load = pltpu.make_async_copy(full_x, x_in, work.at[0])
-    load.start()
-    load.wait()
 
     @pl.loop(0, x_in.shape[1] // 128)
     def _(i):
         at = pl.ds(pl.multiple_of(i * 128, 128), 128)
         xt[at, :] = x_in[:, at].T
 
-    store = pltpu.make_async_copy(xt, xt_out, work.at[1])
+    store = pltpu.make_async_copy(xt, xt_out, work.at[0])
     store.start()
+    project(z, x)
+    both_ways(1, lambda zz, up: project(zz, x))
+
+    @pl.loop(2, depth)
+    def _(d):
+        forward(d)
+        both_ways(d, lambda zz, up: project(zz, x))
+
+        @pl.when(d == 2)
+        def _():
+            take_x(z)
+
+        @pl.when(d > 2)
+        def _():
+            both_ways(d - 2, lambda zz, up: take_x(zz))
+
+    if depth == 2:
+        take_x(z)
+
+    @pl.loop(max(1, depth - 2), depth)
+    def _(d):
+        both_ways(d, lambda zz, up: take_x(zz))
+
+    q_out[...] = acc[0].astype(BF16)
+    k_out[...] = acc[1].astype(BF16)
+
+    for w in range(2):
+        early_x(w).wait_send()
 
     @pl.loop(0, depth)
     def _(zz):
-        for c in range(PARTS):
-            other = piece(zz, 1 - x, c)
-            remote(
-                other, other, x_s.at[zz, c], x_r.at[zz, c], "fsdp", z * 2 + 1 - x
-            ).wait_recv()
-            to_x(own(c), zz, c).wait_send()
+        for w in range(2):
+            for xx in range(2):
+                keep(zz, xx, w).wait()
+        for p in range(PARTS):
+            to_x(own(p), zz, p).wait_send()
+        for p in range(PARTS + 4):
 
             @pl.when((zz <= z) & (z < depth - 1))
             def _():
-                to_up(own(c), zz, c).wait_send()
+                to_z(own(p), zz, p, up_s, 1).wait_send()
 
             @pl.when((zz >= z) & (z > 0))
             def _():
-                to_dn(own(c), zz, c).wait_send()
+                to_z(own(p), zz, p, dn_s, -1).wait_send()
 
     store.wait()
 
 
-def attend_kernel(idx, cnt, x, wq, wk, v, g, grad, grad_v, p_s, d_s):
+def attend_kernel(live_bits, q_in, k_in, v, g, grad, grad_v, p_s, d_s):
     h = pl.program_id(0)
-    nb = idx.shape[2]
-    block = x.shape[0] // nb
+    nb = live_bits.shape[1]
+    block = q_in.shape[0] // nb
     scale = 1.0 / math.sqrt(HEAD_DIM)
-    both = jnp.dot(
-        x[...], jnp.concatenate([wq[...], wk[...]], axis=1), preferred_element_type=F32
-    ).astype(BF16)
-    q, k = both[:, :HEAD_DIM], both[:, HEAD_DIM:]
+    q, k = q_in[...], k_in[...]
     vv, gg = v[...], g[...]
     nt = (((1,), (1,)), ((), ()))
     tn = (((0,), (0,)), ((), ()))
     col = lax.broadcasted_iota(jnp.int32, (block, nb * block), 1) // block
     for i in range(nb):
-        live = jnp.zeros(col.shape, jnp.bool_)
-        for n in range(nb):
-            j = jnp.where(n < cnt[h, i], idx[h, i, n], -1)
-            live = live | (col == j)
+        live = ((live_bits[h, i] >> col) & 1) == 1
         at = slice(i * block, (i + 1) * block)
         scores = lax.dot_general(q[at], k, nt, preferred_element_type=F32) * scale
         scores = jnp.where(live, scores, -jnp.inf)
@@ -234,12 +303,13 @@
 
 def scatter_kernel(
     n_f, n_s, chunk, xt_h, full_q, full_k, grad, gv, gx_out, gv_out, gw_out,
-    xt, wbuf, xsend, xrecv, own, zrecv, gx, gxr,
-    x_s, x_r, z_s, z_r, sp_s, sp_r, work,
+    xt, wbuf, xsend, xrecv, own, zrecv, fown, fzrecv, fxrecv, gx, gxr,
+    x_s, x_r, z_s, z_r, fz_s, fz_r, fx_s, fx_r, sp_s, sp_r, work,
 ):
     depth, z, x, s = place(n_f)
     rows, cols = gw_out.shape[1], gw_out.shape[2]
-    half = rows // 2
+    few = first_rows(rows)
+    half = (rows - few) // 2
     t, width = gx_out.shape
 
     def w_copy(i, slot):
@@ -262,10 +332,26 @@
         w = c // 2
         return w, pl.ds(pl.multiple_of((c % 2) * half, 16), half)
 
+    def main_rows(c):
+        return pl.ds(pl.multiple_of(few + (c % 2) * half, 16), half)
+
+    def product(zz, xx, w, start, size):
+        at = pl.ds(pl.multiple_of((zz * 2 + xx) * rows + start, 16), size)
+        return jnp.dot(xt[at, :], grad[w], preferred_element_type=F32).astype(BF16)
+
     def term(zz, xx, c):
-        start = (zz * 2 + xx) * rows + (c % 2) * half
-        at = pl.ds(pl.multiple_of(start, 16), half)
-        return jnp.dot(xt[at, :], grad[c // 2], preferred_element_type=F32).astype(BF16)
+        return product(zz, xx, c // 2, few + (c % 2) * half, half)
+
+    def early_z(zz, e, slot, target):
+        return remote(
+            fown.at[zz, e], fzrecv.at[slot, e], fz_s.at[zz, e], fz_r.at[slot, e],
+            "fsdp", target * 2 + x,
+        )
+
+    def early_x(w):
+        return remote(
+            fown.at[z, 2 + w], fxrecv.at[w], fx_s.at[w], fx_r.at[w], "fsdp", z * 2 + 1 - x
+        )
 
     def to_x(zz, c):
         w, at = part(c)
@@ -314,12 +400,44 @@
         xsend[zz, w, at, :] = term(zz, 1 - x, c)
         to_x(zz, c).start()
 
+    @pl.loop(0, depth * 4)
+    def _(i):
+        zz, e = order(i // 4), i % 4
+        rel = e // 2
+        fown[zz, e] = product(zz, x + rel * (1 - 2 * x), e % 2, 0, few)
+
+        @pl.when((z == 0) & (zz > z))
+        def _():
+            early_z(zz, e, zz, z + 1).start()
+
+        @pl.when((z == depth - 1) & (zz < z))
+        def _():
+            early_z(zz, e, jnp.where(zz == z - 1, depth, zz), z - 1).start()
+
     @pl.loop(0, depth * PARTS)
     def _(i):
         zz, c = i // PARTS, i % PARTS
         w, at = part(c)
         own[zz, w, at, :] = term(zz, x, c)
 
+    @pl.loop(0, depth * 4)
+    def _(i):
+        zz, e = order(i // 4), i % 4
+        more = ((zz > z) & (z > 0)) | ((zz < z) & (z < depth - 1))
+
+        @pl.when(more)
+        def _():
+            early_z(zz, e, zz, z).wait_recv()
+            fown[zz, e] = (fown[zz, e].astype(F32) + fzrecv[zz, e].astype(F32)).astype(BF16)
+
+        @pl.when((z > 0) & (zz > z))
+        def _():
+            early_z(zz, e, zz, z + 1).start()
+
+        @pl.when((z < depth - 1) & (zz < z))
+        def _():
+            early_z(zz, e, jnp.where(zz == z - 1, depth, zz), z - 1).start()
+
     nt = (((1,), (1,)), ((), ()))
     chunks = width // chunk
 
@@ -340,6 +458,25 @@
 
     for k in range(1, n_s):
         gx_copy(k).start()
+
+    def early_sum(e):
+        @pl.when(z > 0)
+        def _():
+            early_z(z, e, z, z).wait_recv()
+
+        @pl.when(z < depth - 1)
+        def _():
+            early_z(z, e, depth, z).wait_recv()
+
+        below = jnp.where(z > 0, fzrecv[z, e].astype(F32), 0.0)
+        above = jnp.where(z < depth - 1, fzrecv[depth, e].astype(F32), 0.0)
+        return fown[z, e].astype(F32) + below + above
+
+    for w in range(2):
+        fown[z, 2 + w] = early_sum(2 + w).astype(BF16)
+        early_x(w).start()
+    for w in range(2):
+        gw_out[w, :few, :] = early_sum(w)
 
     @pl.loop(0, depth * PARTS)
     def _(i):
@@ -371,7 +508,11 @@
 
         @pl.when(zz == z)
         def _():
-            gw_out[w, at, :] = paired()
+            gw_out[w, main_rows(c), :] = paired()
+
+    for w in range(2):
+        early_x(w).wait_recv()
+        gw_out[w, :few, :] += fxrecv[w].astype(F32)
 
     for k in range(1, n_s):
         gx_copy(k).wait_recv()
@@ -391,12 +532,12 @@
         @pl.when(z > 0)
         def _():
             to_z(z, c, z, z).wait_recv()
-            gw_out[w, at, :] += zrecv[z, w, at, :].astype(F32)
+            gw_out[w, main_rows(c), :] += zrecv[z, w, at, :].astype(F32)
 
         @pl.when(z < depth - 1)
         def _():
             to_z(z, c, depth, z).wait_recv()
-            gw_out[w, at, :] += zrecv[depth, w, at, :].astype(F32)
+            gw_out[w, main_rows(c), :] += zrecv[depth, w, at, :].astype(F32)
 
     @pl.loop(0, depth * PARTS)
     def _(i):
@@ -406,6 +547,10 @@
         @pl.when(zz != z)
         def _():
             to_z(zz, c, zz, z).wait_send()
+            early_z(zz, c, zz, z).wait_send()
+
+    for w in range(2):
+        early_x(w).wait_send()
 
     for k in range(1, n_s):
         gx_copy(k).wait_send()
@@ -424,10 +569,12 @@
     smem = pl.BlockSpec(memory_space=pltpu.SMEM)
     dma = pltpu.SemaphoreType.DMA
     shape = jax.ShapeDtypeStruct
-    full_x, full_q, full_k, full_v, full_g, xt = pl.pallas_call(
+    slots = PARTS + 4
+    q, k, full_q, full_k, full_v, full_g, xt = pl.pallas_call(
         functools.partial(gather_kernel, n_f, n_s),
         out_shape=(
-            shape((length, width), BF16),
+            shape((length, cols), BF16),
+            shape((length, cols), BF16),
             shape((width, cols), BF16),
             shape((width, cols), BF16),
             shape((length, cols), BF16),
@@ -435,19 +582,24 @@
             shape((width, length), BF16),
         ),
         in_specs=[hbm] * 5,
-        out_specs=(hbm,) * 6,
+        out_specs=(vmem, vmem) + (hbm,) * 5,
         scratch_shapes=[
             pltpu.VMEM((length, width), BF16),
             pltpu.VMEM((width, length), BF16),
+            pltpu.VMEM((2, width, cols), BF16),
+            pltpu.VMEM((2, length, cols), F32),
+            dma((depth, slots)),
+            dma((depth, slots)),
+            dma((depth, slots)),
             dma((depth, PARTS)),
             dma((depth, PARTS)),
-            dma((depth, PARTS)),
-            dma((depth, PARTS)),
-            dma((depth, PARTS)),
+            dma((2,)),
+            dma((2,)),
             dma((3, n_s - 1)),
             dma((3, n_s - 1)),
             dma((5,)),
-            dma((2,)),
+            dma((n_f, 2)),
+            dma((1,)),
         ],
         compiler_params=pltpu.CompilerParams(
             collective_id=0, has_side_effects=True, vmem_limit_bytes=60 * 2**20
@@ -455,28 +607,22 @@
         name="gather",
     )(tokens[0], w_query, w_key, values[0], grad_out[0])
 
+    index, count = kv_index[0], kv_count[0]
+    in_use = jnp.arange(index.shape[-1], dtype=jnp.int32) < count[..., None]
+    live_bits = jnp.sum(jnp.where(in_use, 1 << index, 0), axis=-1, dtype=jnp.int32)
+    head = pl.BlockSpec((length, HEAD_DIM), lambda h: (0, h))
     grad, gv = pl.pallas_call(
         attend_kernel,
         grid=(heads,),
         out_shape=(shape((2, length, cols), BF16), shape((length, cols), BF16)),
-        in_specs=[
-            smem,
-            smem,
-            pl.BlockSpec((length, width), lambda h: (0, 0)),
-            pl.BlockSpec((width, HEAD_DIM), lambda h: (0, h)),
-            pl.BlockSpec((width, HEAD_DIM), lambda h: (0, h)),
-            pl.BlockSpec((length, HEAD_DIM), lambda h: (0, h)),
-            pl.BlockSpec((length, HEAD_DIM), lambda h: (0, h)),
-        ],
-        out_specs=(
-            pl.BlockSpec((2, length, HEAD_DIM), lambda h: (0, 0, h)),
-            pl.BlockSpec((length, HEAD_DIM), lambda h: (0, h)),
-        ),
+        in_specs=[smem, head, head, head, head],
+        out_specs=(pl.BlockSpec((2, length, HEAD_DIM), lambda h: (0, 0, h)), head),
         scratch_shapes=[pltpu.VMEM((length, length), BF16), pltpu.VMEM((length, length), BF16)],
         compiler_params=pltpu.CompilerParams(vmem_limit_bytes=60 * 2**20),
         name="attend",
-    )(kv_index[0], kv_count[0], full_x, full_q, full_k, full_v, full_g)
-
+    )(live_bits, q, k, full_v, full_g)
+
+    few = first_rows(rows)
     chunk = 512 if width % 512 == 0 else 128
     gx, token_gv, gw = pl.pallas_call(
         functools.partial(scatter_kernel, n_f, n_s, chunk),
@@ -490,16 +636,23 @@
         scratch_shapes=[
             pltpu.VMEM((width, length), BF16),
             pltpu.VMEM((2, 2, chunk, cols), BF16),
-            pltpu.VMEM((depth, 2, rows, cols), BF16),
-            pltpu.VMEM((depth, 2, rows, cols), BF16),
-            pltpu.VMEM((depth, 2, rows, cols), BF16),
-            pltpu.VMEM((depth + 1, 2, rows, cols), BF16),
+            pltpu.VMEM((depth, 2, rows - few, cols), BF16),
+            pltpu.VMEM((depth, 2, rows - few, cols), BF16),
+            pltpu.VMEM((depth, 2, rows - few, cols), BF16),
+            pltpu.VMEM((depth + 1, 2, rows - few, cols), BF16),
+            pltpu.VMEM((depth, 4, few, cols), BF16),
+            pltpu.VMEM((depth + 1, 4, few, cols), BF16),
+            pltpu.VMEM((2, few, cols), BF16),
             pltpu.VMEM((length, width), BF16),
             pltpu.VMEM((n_s - 1, t, width), BF16),
             dma((depth, PARTS)),
             dma((depth, PARTS)),
             dma((depth, PARTS)),
             dma((depth + 1, PARTS)),
+            dma((depth, 4)),
+            dma((depth + 1, 4)),
+            dma((2,)),
+            dma((2,)),
             dma((2, n_s - 1)),
             dma((2, n_s - 1)),
             dma((3, 2)),

time: 349 us -> 313 us (0.90)
  Pallas kernels: 339 us -> 304 us
    pallas_call x1, Pallas kernels: 23.9 us -> 8.44 us  [local(): pl.pallas_call(attend_kernel, grid=(heads,), out_shape=(shape((2, length,...]
    pallas_call x1, Pallas kernels: 146 us -> 133 us  [local(): pl.pallas_call(functools.partial(gather_kernel, n_f, n_s), out_shape=(sha...]
    pallas_call x1, Pallas kernels: 169 us -> 162 us  [local(): pl.pallas_call(functools.partial(scatter_kernel, n_f, n_s, chunk), out_sh...]
where the time goes in v2:
time: 313 us; the launch traced here: 312 us
  Pallas kernels  304 us (97%)
  local copies, waits for them, and re-layouts  6.97 us (2%)
    pallas_call x1, Pallas kernels, local(): pl.pallas_call(functools.partial(scatter_kernel, n_f, n_s, chunk), out_sh...  162 us
    pallas_call x1, Pallas kernels, local(): pl.pallas_call(functools.partial(gather_kernel, n_f, n_s), out_shape=(sha...  133 us
    pallas_call x1, Pallas kernels, local(): pl.pallas_call(attend_kernel, grid=(heads,), out_shape=(shape((2, length,...  8.44 us

profile of v2, /device:TPU:8, one launch (start us, length us, event | category | flops | bytes accessed | tf_op | source)
XLA Modules:
  0.0 312.3 jit_solution(15256828913881234314)
XLA Ops:
  0.6 0.7 fusion
  1.4 0.7 copy.11.live_bits
  2.0 133.1 %gather.1 = (bf16[512,640]{1,0:T(8,128)(2,1)}, bf16[512,640]{1,0:T(8,128)(2,1)}, bf16[5120,640]{1,0:T(8,128)(2,1)}, bf16[5120,640]{1,0:T(8,128)(2,1)}, bf16[512,...) custom-call(bf16[128,5120]{1,0:T(8,128)(2,1)} %bitcast.14, bf16[640,640]{1,0:T(8,128)(2,1)} %wq.1, ...), custom_call_target="tpu_custom_call" | custom-call | tf_op jit(solution)/shard_map/gather/pallas_call | solution.py:573
  135.2 8.4 %attend.1 = (bf16[2,512,640]{2,1,0:T(8,128)(2,1)}, bf16[512,640]{1,0:T(8,128)(2,1)}) custom-call(s32[5,4]{1,0:T(8,128)} %copy.11.live_bits, bf16[512,640]{1,0:T(8,128)(2,1)} %get-tuple-element.19.q_in, bf16[512,640]{1,0:T(8,128)(2,1)} %get-tuple-element.20.k_in, bf16[512,640]{1,0:T(8,128)(2,1)} %get-tuple-element.21.v, bf16[512,640]{1,0:T(8,128)(2,1)} %get-tuple-element.22.g), custom_call_target="tpu_custom_call" | custom-call | tf_op jit(solution)/shard_map/attend/pallas_call | solution.py:614
  143.6 162.4 %scatter.1 = (bf16[128,5120]{1,0:T(8,128)(2,1)}, bf16[128,2560]{1,0:T(8,128)(2,1)}, f32[2,640,640]{2,1,0:T(8,128)}) custom-call(bf16[5120,512]{1,0:T(8,128)(2,1)} %get-tuple-element.16.xt_h, bf16[5120,640]{1,0:T(8,128)(2,1)} %get-tuple-element.17.full_q, bf16[5120,640]{1,0:T(8,128)(2,1)} %get-tuple-element.18.full_k, ...), custom_call_target="tpu_custom_call" | custom-call | tf_op jit(solution)/shard_map/scatter/pallas_call | solution.py:627
  306.0 0.0 copy-start
  306.0 3.9 %slice_bitcast_fusion = (f32[640,640]{1,0:T(8,128)}, f32[640,640]{1,0:T(8,128)}) fusion(f32[2,640,640]{2,1,0:T(8,128)} %get-tuple-element.27), kind=kLoop, calls=%fused_computation | loop fusion | bytes 6553600 | tf_op jit(solution)/shard_map/squeeze | solution.py:665
  310.0 0.0 copy-start.1
  310.0 0.0 copy-done
  310.0 1.1 copy.14
  311.0 0.5 copy-done.1
  311.5 0.8 copy.15
Async XLA Ops:
  306.0 4.0 %copy-start = (bf16[128,5120]{1,0:T(8,128)(2,1)S(1)}, bf16[128,5120]{1,0:T(8,128)(2,1)}, u32[]{:S(2)}) copy-start(bf16[128,5120]{1,0:T(8,128)(2,1)} %get-tuple-element.25) | copy-start | bytes 3932164
  310.0 1.5 copy-start.1

commit v3 on v2

--- a/solution.py
+++ b/solution.py
@@ -62,7 +62,7 @@
 
 def gather_kernel(
     n_f, n_s, tok, wq, wk, val, gout, q_out, k_out, full_q, full_k, full_v, full_g, xt_out,
-    x_in, xt, land, acc, up_s, dn_s, z_r, x_s, x_r, xf_s, xf_r, sp_s, sp_r, loc, out_sem, work,
+    x_in, xt, land, acc, up_s, dn_s, z_r, x_s, x_r, xf_s, xf_r, tok_s, tok_r, sp_s, sp_r, loc, out_sem, work,
 ):
     depth, z, x, s = place(n_f)
     rows = wq.shape[0]
@@ -126,12 +126,27 @@
             remote(src, dst, sp_s.at[i, k - 1], sp_r.at[i, k - 1], "sp", j)
             for i, (src, dst) in enumerate(
                 (
-                    (tok, x_in.at[mine]),
                     (val.at[:, cols], full_v.at[mine]),
                     (gout.at[:, cols], full_g.at[mine]),
                 )
             )
         ]
+
+    pairs, mate = n_s // 2, s + 1 - 2 * (s % 2)
+
+    def tok_at(owner):
+        return x_in.at[pl.ds(pl.multiple_of(owner * t, 16), t)]
+
+    def friend(k):
+        return ((s // 2 + k) % pairs) * 2 + s % 2
+
+    def tok_direct(k):
+        target = mate if k == 0 else friend(k)
+        return remote(tok, tok_at(s), tok_s.at[k], tok_r.at[s], "sp", target)
+
+    def tok_relay(owner, k):
+        blk = tok_at(owner)
+        return remote(blk, blk, tok_s.at[pairs - 1 + k], tok_r.at[owner], "sp", mate)
 
     locals_ = [
         pltpu.make_async_copy(src, dst, loc.at[i])
@@ -153,6 +168,8 @@
         send_z(own(p), z, p, True, True)
     for w in range(2):
         send_z(own(PARTS + w), z, PARTS + w, True, True)
+    for k in range(pairs):
+        tok_direct(k).start()
     for k in range(1, n_s):
         for copy in sp_copies(k):
             copy.start()
@@ -212,45 +229,54 @@
         project(zz, 1 - x)
 
     forward(1)
+    for k in range(1, pairs):
+        tok_relay(friend(k), k).wait_recv()
+        tok_relay(friend(k), k).start()
+    for copy in locals_:
+        copy.wait()
+    for k in range(pairs):
+        tok_relay(friend(k) + 1 - 2 * (s % 2), k).wait_recv()
+
+    @pl.loop(0, x_in.shape[1] // 128)
+    def _(i):
+        at = pl.ds(pl.multiple_of(i * 128, 128), 128)
+        xt[at, :] = x_in[:, at].T
+
+    store = pltpu.make_async_copy(xt, xt_out, work.at[0])
+    store.start()
+    project(z, x)
+
+    @pl.loop(2, depth)
+    def _(d):
+        forward(d)
+        both_ways(d - 1, lambda zz, up: project(zz, x))
+
+        @pl.when(d == 2)
+        def _():
+            take_x(z)
+
+        @pl.when(d > 2)
+        def _():
+            both_ways(d - 2, lambda zz, up: take_x(zz))
+
+    both_ways(depth - 1, lambda zz, up: project(zz, x))
+    if depth == 2:
+        take_x(z)
+
+    @pl.loop(max(1, depth - 2), depth)
+    def _(d):
+        both_ways(d, lambda zz, up: take_x(zz))
+
+    q_out[...] = acc[0].astype(BF16)
+    k_out[...] = acc[1].astype(BF16)
+
     for k in range(1, n_s):
         for copy in sp_copies(k):
             copy.wait()
-    for copy in locals_:
-        copy.wait()
-
-    @pl.loop(0, x_in.shape[1] // 128)
-    def _(i):
-        at = pl.ds(pl.multiple_of(i * 128, 128), 128)
-        xt[at, :] = x_in[:, at].T
-
-    store = pltpu.make_async_copy(xt, xt_out, work.at[0])
-    store.start()
-    project(z, x)
-    both_ways(1, lambda zz, up: project(zz, x))
-
-    @pl.loop(2, depth)
-    def _(d):
-        forward(d)
-        both_ways(d, lambda zz, up: project(zz, x))
-
-        @pl.when(d == 2)
-        def _():
-            take_x(z)
-
-        @pl.when(d > 2)
-        def _():
-            both_ways(d - 2, lambda zz, up: take_x(zz))
-
-    if depth == 2:
-        take_x(z)
-
-    @pl.loop(max(1, depth - 2), depth)
-    def _(d):
-        both_ways(d, lambda zz, up: take_x(zz))
-
-    q_out[...] = acc[0].astype(BF16)
-    k_out[...] = acc[1].astype(BF16)
-
+    for k in range(pairs):
+        tok_direct(k).wait_send()
+    for k in range(1, pairs):
+        tok_relay(friend(k), k).wait_send()
     for w in range(2):
         early_x(w).wait_send()
 
@@ -595,8 +621,10 @@
             dma((depth, PARTS)),
             dma((2,)),
             dma((2,)),
-            dma((3, n_s - 1)),
-            dma((3, n_s - 1)),
+            dma((n_s - 1,)),
+            dma((n_s,)),
+            dma((2, n_s - 1)),
+            dma((2, n_s - 1)),
             dma((5,)),
             dma((n_f, 2)),
             dma((1,)),

time: 313 us -> 299 us (0.955)
  Pallas kernels: 304 us -> 290 us
    pallas_call x1, Pallas kernels: 162 us -> 148 us  [local(): pl.pallas_call(functools.partial(scatter_kernel, n_f, n_s, chunk), out_sh...]
where the time goes in v3:
time: 299 us; the launch traced here: 298 us
  Pallas kernels  290 us (97%)
  local copies, waits for them, and re-layouts  6.97 us (2%)
    pallas_call x1, Pallas kernels, local(): pl.pallas_call(functools.partial(scatter_kernel, n_f, n_s, chunk), out_sh...  148 us
    pallas_call x1, Pallas kernels, local(): pl.pallas_call(functools.partial(gather_kernel, n_f, n_s), out_shape=(sha...  133 us
    pallas_call x1, Pallas kernels, local(): pl.pallas_call(attend_kernel, grid=(heads,), out_shape=(shape((2, length,...  8.44 us

profile of v3, /device:TPU:8, one launch (start us, length us, event | category | flops | bytes accessed | tf_op | source)
XLA Modules:
  0.0 298.2 jit_solution(14397044816726032600)
XLA Ops:
  0.6 0.7 fusion
  1.4 0.7 copy.11.live_bits
  2.0 133.1 %gather.1 = (bf16[512,640]{1,0:T(8,128)(2,1)}, bf16[512,640]{1,0:T(8,128)(2,1)}, bf16[5120,640]{1,0:T(8,128)(2,1)}, bf16[5120,640]{1,0:T(8,128)(2,1)}, bf16[512,...) custom-call(bf16[128,5120]{1,0:T(8,128)(2,1)} %bitcast.14, bf16[640,640]{1,0:T(8,128)(2,1)} %wq.1, ...), custom_call_target="tpu_custom_call" | custom-call | tf_op jit(solution)/shard_map/gather/pallas_call | solution.py:599
  135.2 8.4 %attend.1 = (bf16[2,512,640]{2,1,0:T(8,128)(2,1)}, bf16[512,640]{1,0:T(8,128)(2,1)}) custom-call(s32[5,4]{1,0:T(8,128)} %copy.11.live_bits, bf16[512,640]{1,0:T(8,128)(2,1)} %get-tuple-element.19.q_in, bf16[512,640]{1,0:T(8,128)(2,1)} %get-tuple-element.20.k_in, bf16[512,640]{1,0:T(8,128)(2,1)} %get-tuple-element.21.v, bf16[512,640]{1,0:T(8,128)(2,1)} %get-tuple-element.22.g), custom_call_target="tpu_custom_call" | custom-call | tf_op jit(solution)/shard_map/attend/pallas_call | solution.py:642
  143.6 148.3 %scatter.1 = (bf16[128,5120]{1,0:T(8,128)(2,1)}, bf16[128,2560]{1,0:T(8,128)(2,1)}, f32[2,640,640]{2,1,0:T(8,128)}) custom-call(bf16[5120,512]{1,0:T(8,128)(2,1)} %get-tuple-element.16.xt_h, bf16[5120,640]{1,0:T(8,128)(2,1)} %get-tuple-element.17.full_q, bf16[5120,640]{1,0:T(8,128)(2,1)} %get-tuple-element.18.full_k, ...), custom_call_target="tpu_custom_call" | custom-call | tf_op jit(solution)/shard_map/scatter/pallas_call | solution.py:655
  291.9 0.0 copy-start
  291.9 3.9 %slice_bitcast_fusion = (f32[640,640]{1,0:T(8,128)}, f32[640,640]{1,0:T(8,128)}) fusion(f32[2,640,640]{2,1,0:T(8,128)} %get-tuple-element.27), kind=kLoop, calls=%fused_computation | loop fusion | bytes 6553600 | tf_op jit(solution)/shard_map/squeeze | solution.py:693
  295.9 0.0 copy-start.1
  295.9 0.0 copy-done
  295.9 1.1 copy.14
  296.9 0.5 copy-done.1
  297.4 0.8 copy.15
Async XLA Ops:
  291.9 4.0 %copy-start = (bf16[128,5120]{1,0:T(8,128)(2,1)S(1)}, bf16[128,5120]{1,0:T(8,128)(2,1)}, u32[]{:S(2)}) copy-start(bf16[128,5120]{1,0:T(8,128)(2,1)} %get-tuple-element.25) | copy-start | bytes 3932164
  295.9 1.5 copy-start.1
